TPU v7x, 512 devices: a whole 4x4x16 slice. The times are simulated.
512 devices in a mesh: ang: 4 (over y), gy: 32 (over z_lo, x, core), gx: 4 (over z_hi).
Axes of the slice: x: 4, y: 4, z: 16 (z_hi: 4, z_lo: 4; z = z_hi * 4 + z_lo), core: 2. Of those that a mesh axis runs over, the one named last changes fastest.
Arguments:
- spectrum_data: bfloat16 [2, 16, 256, 2048], P(None, None, 'gy', 'ang'), may hold values from -6 to 6
- offsets: int32 [2048], P('ang'), may hold values from 0 to 1020
- view_index: int32 [2048], P('ang'), may hold values from 0 to 1499
- kernel: float32 [4, 2048], P(None, 'ang'), may hold values from 0.25 to 1
- view_weight: float32 [1500], replicated, may hold values from 0.5 to 2
- volume: float32 [16, 256, 4096], P('ang', 'gy', 'gx'), may hold values from -6 to 6
- multiplier: float32 [16, 256, 4096], P('ang', 'gy', 'gx'), may hold values from -4 to 4
Outputs:
- denoised: float32 [16, 256, 4096], P('ang', 'gy', 'gx')
Inputs may be any that keep to these rules, and one draw needn't show every extreme that they name: `offsets`: each offset is a cell of its sample's block of 1024 frequencies with the three cells after it in the block too.
All inputs are finite; a program needn't handle non-finite values.
Results may differ from a plain program's by a relative error of at most 0.0032.
Values sent between devices are 32-bit elements; how exact they have to be, the bound alone decides.
A program may use at most 64 MiB of HBM per device.

v0:
```python
import math

import jax
import jax.numpy as jnp
from jax import lax
from jax.sharding import PartitionSpec as P

NX = 4096
TV_STEPS = 4


smooth_weight = 0.5
dual_step = 1.0 / 12.0


def cut_along(shard, dim, length):
    before, after = (shard.shape[:dim], shard.shape[dim + 1 :])
    return jnp.moveaxis(shard.reshape(*before, length, -1, *after), dim, 0)


def summed_on_arrival(shard, axis, dim):
    blocks = cut_along(shard, dim, lax.axis_size(axis))
    arrived = lax.all_to_all(blocks, axis, split_axis=0, concat_axis=0, tiled=True)
    return arrived.sum(axis=0)


def passed_along(block, axis, distance):
    devices = range(lax.axis_size(axis))
    route = [(i - distance, i) for i in devices if i - distance in devices]
    return lax.ppermute(block, axis, route)


def wave_table(freq_first, freq_count, cell_first, cell_count):
    freq_ids = freq_first + jnp.arange(freq_count, dtype=jnp.int32)
    cell_ids = cell_first + jnp.arange(cell_count, dtype=jnp.int32)
    phase_cells = freq_ids[:, None] * cell_ids[None, :] % NX
    phase_angle = phase_cells.astype(jnp.float32) * (2.0 * math.pi / NX)
    return jnp.concatenate([jnp.cos(phase_angle), -jnp.sin(phase_angle)], axis=0).astype(
        jnp.bfloat16
    )


def spread_block(offsets, view_index, kernel, view_weight, block_size):
    cell_ids = jnp.arange(block_size, dtype=jnp.int32)
    spread_sum = jnp.zeros((offsets.shape[0], block_size), jnp.float32)
    for tap_index in range(kernel.shape[0]):
        spread_sum = spread_sum + jnp.where(
            cell_ids[None, :] == (offsets + tap_index)[:, None],
            kernel[tap_index][:, None],
            jnp.float32(0.0),
        )
    view_ids = jnp.arange(view_weight.shape[0], dtype=jnp.int32)
    weights = jnp.sum(
        jnp.where(view_index[:, None] == view_ids[None, :], view_weight[None, :], jnp.float32(0.0)),
        axis=1,
    )
    return (weights[:, None] * spread_sum).astype(jnp.bfloat16)


def per_device(spectrum_data, offsets, view_index, kernel, view_weight, volume, multiplier):
    block_size = NX // lax.axis_size("ang")
    planes, line_count, columns = volume.shape
    spread = spread_block(offsets, view_index, kernel, view_weight, block_size)
    wave_rows = wave_table(
        lax.axis_index("ang") * block_size, block_size, lax.axis_index("gx") * columns, columns
    )
    row_count = planes * lax.axis_size("ang")
    flat_rows = row_count * line_count
    gridded = jnp.dot(
        spectrum_data.reshape(2 * flat_rows, spectrum_data.shape[3]),
        spread,
        preferred_element_type=jnp.float32,
    ).astype(jnp.bfloat16)
    joined = jnp.concatenate([gridded[:flat_rows], gridded[flat_rows:]], axis=1)
    back = summed_on_arrival(
        jnp.dot(joined, wave_rows, preferred_element_type=jnp.float32).reshape(
            row_count, line_count, columns
        ),
        "ang",
        0,
    )
    back = back * NX ** (-0.5)
    source = volume - back + multiplier
    scaled = source / smooth_weight
    plane_end = (
        lax.axis_index("ang") * planes + jnp.arange(planes, dtype=jnp.int32)
        == planes * lax.axis_size("ang") - 1
    )
    row_end = (
        lax.axis_index("gy") * line_count + jnp.arange(line_count, dtype=jnp.int32)
        == line_count * lax.axis_size("gy") - 1
    )
    cell_end = (
        lax.axis_index("gx") * columns + jnp.arange(columns, dtype=jnp.int32)
        == columns * lax.axis_size("gx") - 1
    )
    flow_field = jnp.zeros((3, planes, line_count, columns), jnp.float32)
    for repeat in range(TV_STEPS + 1):
        lower_plane = passed_along(flow_field[0, -1:], "ang", 1)
        lower_row = passed_along(flow_field[1, :, -1:], "gy", 1)
        lower_cell = passed_along(flow_field[2, :, :, -1:], "gx", 1)
        plane_part = flow_field[0] - jnp.concatenate([lower_plane, flow_field[0, :-1]], axis=0)
        row_part = flow_field[1] - jnp.concatenate([lower_row, flow_field[1, :, :-1]], axis=1)
        cell_part = flow_field[2] - jnp.concatenate([lower_cell, flow_field[2, :, :, :-1]], axis=2)
        local_div = plane_part + row_part + cell_part
        if repeat == TV_STEPS:
            return source - smooth_weight * local_div
        target = local_div - scaled
        upper_plane = passed_along(target[:1], "ang", -1)
        upper_row = passed_along(target[:, :1], "gy", -1)
        upper_cell = passed_along(target[:, :, :1], "gx", -1)
        slope_plane = jnp.where(
            plane_end[:, None, None],
            jnp.float32(0.0),
            jnp.concatenate([target[1:], upper_plane], axis=0) - target,
        )
        slope_row = jnp.where(
            row_end[None, :, None],
            jnp.float32(0.0),
            jnp.concatenate([target[:, 1:], upper_row], axis=1) - target,
        )
        slope_cell = jnp.where(
            cell_end[None, None, :],
            jnp.float32(0.0),
            jnp.concatenate([target[:, :, 1:], upper_cell], axis=2) - target,
        )
        slope_norm = jnp.sqrt(
            slope_plane * slope_plane + slope_row * slope_row + slope_cell * slope_cell
        )
        flow_field = (flow_field + dual_step * jnp.stack([slope_plane, slope_row, slope_cell])) / (
            1.0 + dual_step * slope_norm
        )
    return source


def solution(mesh):
    placed = (
        P(None, None, "gy", "ang"),
        P("ang"),
        P("ang"),
        P(None, "ang"),
        P(),
        P("ang", "gy", "gx"),
        P("ang", "gy", "gx"),
    )
    return jax.shard_map(
        per_device, mesh=mesh, in_specs=placed, out_specs=P("ang", "gy", "gx"), check_vma=False
    )
```

profile of v0, /device:TPU:7, one launch (start us, length us, event | category | flops | bytes accessed | tf_op | source)
XLA Modules:
  0.0 175.2 jit_solution(11653559445374535060)
XLA Ops:
  0.0 0.9 fusion.80
  0.9 0.7 broadcast_add_fusion.2
  1.5 1.1 select_reduce_fusion
  2.7 2.2 %fusion.7 = bf16[256,1024]{0,1:T(8,128)(2,1)S(1)} fusion(bf16[256,512]{1,0:T(8,128)(2,1)S(1)} %bitcast.167, f32[512]{0:T(512)S(1)} %bitcast.174, s32[512]{0:T(512)S(1)} %get-tuple-element.32, f32[512]{0:T(512)S(1)} %bitcast.175, s32[512]{0:T(512)S(1)} %get-tuple-element.33, f32[512]{0:T(512)S(1)} %bitcast.173, s32[512]{0:T(512)S(1)} %get-tuple-element.31, ...), kind=kOutput, calls=%fused_computation.22 | convolution fusion | flops 275513344 | bytes 804864 | tf_op jit(solution)/shard_map/dot_general | solution.py:69
  5.0 17.4 %cosine_convert_fusion = (bf16[1024,1024]{1,0:T(8,128)(2,1)S(1)}, bf16[1024,1024]{1,0:T(8,128)(2,1)S(1)}) fusion(s32[1024]{0:T(1024)S(1)} %get-tuple-element.34, s32[1024]{0:T(1024)S(1)} %get-tuple-element.35), kind=kLoop, calls=%fused_computation.13 | loop fusion | flops 17825792 | bytes 4202496 | tf_op jit(solution)/shard_map/convert
  22.5 1.6 fusion.3
  24.0 4.2 %all-to-all-start = ((f32[4,4,8,1024]{3,2,1,0:T(8,128)}), f32[4,4,8,1024]{3,2,1,0:T(8,128)S(1)}, u32[]{:S(2)}, u32[]{:S(2)}) async-start(f32[4,4,8,1024]{3,2,1,0:T(8,128)} %bitcast.6), calls=%async_computation | async-start | bytes 1048576 | tf_op jit(solution)/shard_map/all_to_all | solution.py:23
  28.2 3.4 %collective-permute-start = (f32[1,8,1024]{2,1,0:T(8,128)S(1)}, f32[1,8,1024]{2,1,0:T(8,128)S(1)}, u32[]{:S(2)}, u32[]{:S(2)}) collective-permute-start(f32[1,8,1024]{2,1,0:T(8,128)S(1)} %squeeze.120), channel_id=1, source_target_pairs={{0,128},{128,256},{256,384},{1,129},{129,257},{257,385},{2,130},{1... | collective-permute-start | bytes 98312 | tf_op jit(solution)/shard_map/ppermute | solution.py:30
  31.6 4.9 %collective-permute-start.1 = (f32[4,1,1024]{2,1,0:T(1,128)S(1)}, f32[4,1,1024]{2,1,0:T(1,128)S(1)}, u32[]{:S(2)}, u32[]{:S(2)}) collective-permute-start(f32[4,1,1024]{2,1,0:T(1,128)S(1)} %squeeze.121), channel_id=1, source_target_pairs={{0,4},{4,8},{8,12},{12,16},{16,20},{20,24},{24,28},{28,32},{32,36}... | collective-permute-start | bytes 49160 | tf_op jit(solution)/shard_map/ppermute | solution.py:30
  36.5 8.8 %collective-permute-start.2 = (f32[4,8,1]{2,1,0:T(8,128)S(1)}, f32[4,8,1]{2,1,0:T(8,128)S(1)}, u32[]{:S(2)}, u32[]{:S(2)}) collective-permute-start(f32[4,8,1]{2,1,0:T(8,128)S(1)} %squeeze.122), channel_id=1, source_target_pairs={{0,1},{1,2},{2,3},{4,5},{5,6},{6,7},{8,9},{9,10},{10,11},{12,13},{... | collective-permute-start | bytes 392 | tf_op jit(solution)/shard_map/ppermute | solution.py:30
  45.4 0.8 collective-permute-done.2
  46.3 1.3 collective-permute-start.3
  47.6 1.9 %collective-permute-start.4 = (f32[4,1,1024]{2,1,0:T(1,128)S(1)}, f32[4,1,1024]{2,1,0:T(1,128)S(1)}, u32[]{:S(2)}, u32[]{:S(2)}) collective-permute-start(f32[4,1,1024]{2,1,0:T(1,128)S(1)} %slice.269), channel_id=1, source_target_pairs={{4,0},{8,4},{12,8},{16,12},{20,16},{24,20},{28,24},{32,28},{36,32}... | collective-permute-start | bytes 49160 | tf_op jit(solution)/shard_map/ppermute | solution.py:30
  49.6 1.3 collective-permute-start.5
  51.0 7.9 %collective-permute-done.5 = f32[4,8,1]{2,1,0:T(8,128)S(1)} collective-permute-done((f32[4,8,1]{2,1,0:T(8,128)S(1)}, f32[4,8,1]{2,1,0:T(8,128)S(1)}, u32[]{:S(2)}, u32[]{:S(2)}) %collective-permute-start.5) | collective-permute-done | bytes 160 | tf_op jit(solution)/shard_map/ppermute | solution.py:30
  58.9 0.2 multiply_add_fusion.3
  59.4 4.3 %collective-permute-start.6 = (f32[1,8,1024]{2,1,0:T(8,128)S(1)}, f32[1,8,1024]{2,1,0:T(8,128)S(1)}, u32[]{:S(2)}, u32[]{:S(2)}) collective-permute-start(f32[1,8,1024]{2,1,0:T(8,128)S(1)} %slice_bitcast_fusion.27), channel_id=1, source_target_pairs={{0,128},{128,256},{256,384},{1,129},{129,257},{257,385},{2,130},{1... | collective-permute-start | bytes 98312 | tf_op jit(solution)/shard_map/ppermute | solution.py:30
  63.6 6.4 %collective-permute-start.7 = (f32[4,1,1024]{2,1,0:T(1,128)S(1)}, f32[4,1,1024]{2,1,0:T(1,128)S(1)}, u32[]{:S(2)}, u32[]{:S(2)}) collective-permute-start(f32[4,1,1024]{2,1,0:T(1,128)S(1)} %slice_bitcast_fusion.31), channel_id=1, source_target_pairs={{0,4},{4,8},{8,12},{12,16},{16,20},{20,24},{24,28},{28,32},{32,36}... | collective-permute-start | bytes 49160 | tf_op jit(solution)/shard_map/ppermute | solution.py:30
  70.1 7.9 %collective-permute-start.8 = (f32[4,8,1]{1,0,2:T(4,128)S(1)}, f32[4,8,1]{1,0,2:T(4,128)S(1)}, u32[]{:S(2)}, u32[]{:S(2)}) collective-permute-start(f32[4,8,1]{1,0,2:T(4,128)S(1)} %bitcast.168), channel_id=1, source_target_pairs={{0,1},{1,2},{2,3},{4,5},{5,6},{6,7},{8,9},{9,10},{10,11},{12,13},{... | collective-permute-start | bytes 392 | tf_op jit(solution)/shard_map/ppermute | solution.py:30
  78.0 0.7 collective-permute-done.8
  78.9 1.3 collective-permute-start.9
  80.3 1.9 %collective-permute-start.10 = (f32[4,1,1024]{2,1,0:T(1,128)S(1)}, f32[4,1,1024]{2,1,0:T(1,128)S(1)}, u32[]{:S(2)}, u32[]{:S(2)}) collective-permute-start(f32[4,1,1024]{2,1,0:T(1,128)S(1)} %slice.284), channel_id=1, source_target_pairs={{4,0},{8,4},{12,8},{16,12},{20,16},{24,20},{28,24},{32,28},{36,32}... | collective-permute-start | bytes 49160 | tf_op jit(solution)/shard_map/ppermute | solution.py:30
  82.2 1.3 collective-permute-start.11
  83.6 7.6 %collective-permute-done.11 = f32[4,8,1]{2,1,0:T(8,128)S(1)} collective-permute-done((f32[4,8,1]{2,1,0:T(8,128)S(1)}, f32[4,8,1]{2,1,0:T(8,128)S(1)}, u32[]{:S(2)}, u32[]{:S(2)}) %collective-permute-start.11) | collective-permute-done | bytes 160 | tf_op jit(solution)/shard_map/ppermute | solution.py:30
  91.2 0.2 multiply_add_fusion.2
  91.7 4.0 %collective-permute-start.12 = (f32[1,8,1024]{2,1,0:T(8,128)S(1)}, f32[1,8,1024]{2,1,0:T(8,128)S(1)}, u32[]{:S(2)}, u32[]{:S(2)}) collective-permute-start(f32[1,8,1024]{2,1,0:T(8,128)S(1)} %slice_bitcast_fusion.26), channel_id=1, source_target_pairs={{0,128},{128,256},{256,384},{1,129},{129,257},{257,385},{2,130},{1... | collective-permute-start | bytes 98312 | tf_op jit(solution)/shard_map/ppermute | solution.py:30
  95.7 6.6 %collective-permute-start.13 = (f32[4,1,1024]{2,1,0:T(1,128)S(1)}, f32[4,1,1024]{2,1,0:T(1,128)S(1)}, u32[]{:S(2)}, u32[]{:S(2)}) collective-permute-start(f32[4,1,1024]{2,1,0:T(1,128)S(1)} %slice_bitcast_fusion.30), channel_id=1, source_target_pairs={{0,4},{4,8},{8,12},{12,16},{16,20},{20,24},{24,28},{28,32},{32,36}... | collective-permute-start | bytes 49160 | tf_op jit(solution)/shard_map/ppermute | solution.py:30
  102.3 7.5 %collective-permute-start.14 = (f32[4,8,1]{1,0,2:T(4,128)S(1)}, f32[4,8,1]{1,0,2:T(4,128)S(1)}, u32[]{:S(2)}, u32[]{:S(2)}) collective-permute-start(f32[4,8,1]{1,0,2:T(4,128)S(1)} %bitcast.169), channel_id=1, source_target_pairs={{0,1},{1,2},{2,3},{4,5},{5,6},{6,7},{8,9},{9,10},{10,11},{12,13},{... | collective-permute-start | bytes 392 | tf_op jit(solution)/shard_map/ppermute | solution.py:30
  109.9 0.7 collective-permute-done.14
  110.8 1.3 collective-permute-start.15
  112.1 1.9 %collective-permute-start.16 = (f32[4,1,1024]{2,1,0:T(1,128)S(1)}, f32[4,1,1024]{2,1,0:T(1,128)S(1)}, u32[]{:S(2)}, u32[]{:S(2)}) collective-permute-start(f32[4,1,1024]{2,1,0:T(1,128)S(1)} %slice.299), channel_id=1, source_target_pairs={{4,0},{8,4},{12,8},{16,12},{20,16},{24,20},{28,24},{32,28},{36,32}... | collective-permute-start | bytes 49160 | tf_op jit(solution)/shard_map/ppermute | solution.py:30
  114.1 1.3 collective-permute-start.17
  115.5 7.2 %collective-permute-done.17 = f32[4,8,1]{2,1,0:T(8,128)S(1)} collective-permute-done((f32[4,8,1]{2,1,0:T(8,128)S(1)}, f32[4,8,1]{2,1,0:T(8,128)S(1)}, u32[]{:S(2)}, u32[]{:S(2)}) %collective-permute-start.17) | collective-permute-done | bytes 160 | tf_op jit(solution)/shard_map/ppermute | solution.py:30
  122.7 0.2 multiply_add_fusion.1
  123.3 4.0 %collective-permute-start.18 = (f32[1,8,1024]{2,1,0:T(8,128)S(1)}, f32[1,8,1024]{2,1,0:T(8,128)S(1)}, u32[]{:S(2)}, u32[]{:S(2)}) collective-permute-start(f32[1,8,1024]{2,1,0:T(8,128)S(1)} %slice_bitcast_fusion.25), channel_id=1, source_target_pairs={{0,128},{128,256},{256,384},{1,129},{129,257},{257,385},{2,130},{1... | collective-permute-start | bytes 98312 | tf_op jit(solution)/shard_map/ppermute | solution.py:30
  127.2 6.9 %collective-permute-start.19 = (f32[4,1,1024]{2,1,0:T(1,128)S(1)}, f32[4,1,1024]{2,1,0:T(1,128)S(1)}, u32[]{:S(2)}, u32[]{:S(2)}) collective-permute-start(f32[4,1,1024]{2,1,0:T(1,128)S(1)} %slice_bitcast_fusion.29), channel_id=1, source_target_pairs={{0,4},{4,8},{8,12},{12,16},{16,20},{20,24},{24,28},{28,32},{32,36}... | collective-permute-start | bytes 49160 | tf_op jit(solution)/shard_map/ppermute | solution.py:30
  134.2 7.5 %collective-permute-start.20 = (f32[4,8,1]{1,0,2:T(4,128)S(1)}, f32[4,8,1]{1,0,2:T(4,128)S(1)}, u32[]{:S(2)}, u32[]{:S(2)}) collective-permute-start(f32[4,8,1]{1,0,2:T(4,128)S(1)} %bitcast.170), channel_id=1, source_target_pairs={{0,1},{1,2},{2,3},{4,5},{5,6},{6,7},{8,9},{9,10},{10,11},{12,13},{... | collective-permute-start | bytes 392 | tf_op jit(solution)/shard_map/ppermute | solution.py:30
  141.7 0.7 collective-permute-done.20
  142.7 1.3 collective-permute-start.21
  144.0 1.9 %collective-permute-start.22 = (f32[4,1,1024]{2,1,0:T(1,128)S(1)}, f32[4,1,1024]{2,1,0:T(1,128)S(1)}, u32[]{:S(2)}, u32[]{:S(2)}) collective-permute-start(f32[4,1,1024]{2,1,0:T(1,128)S(1)} %slice.314), channel_id=1, source_target_pairs={{4,0},{8,4},{12,8},{16,12},{20,16},{24,20},{28,24},{32,28},{36,32}... | collective-permute-start | bytes 49160 | tf_op jit(solution)/shard_map/ppermute | solution.py:30
  145.9 1.3 collective-permute-start.23
  147.3 7.2 %collective-permute-done.23 = f32[4,8,1]{2,1,0:T(8,128)S(1)} collective-permute-done((f32[4,8,1]{2,1,0:T(8,128)S(1)}, f32[4,8,1]{2,1,0:T(8,128)S(1)}, u32[]{:S(2)}, u32[]{:S(2)}) %collective-permute-start.23) | collective-permute-done | bytes 160 | tf_op jit(solution)/shard_map/ppermute | solution.py:30
  154.7 0.2 fusion.27
  155.2 4.0 %collective-permute-start.24 = (f32[1,8,1024]{2,1,0:T(8,128)S(1)}, f32[1,8,1024]{2,1,0:T(8,128)S(1)}, u32[]{:S(2)}, u32[]{:S(2)}) collective-permute-start(f32[1,8,1024]{2,1,0:T(8,128)S(1)} %slice_bitcast_fusion.24), channel_id=1, source_target_pairs={{0,128},{128,256},{256,384},{1,129},{129,257},{257,385},{2,130},{1... | collective-permute-start | bytes 98312 | tf_op jit(solution)/shard_map/ppermute | solution.py:30
  159.2 6.9 %collective-permute-start.25 = (f32[4,1,1024]{2,1,0:T(1,128)S(1)}, f32[4,1,1024]{2,1,0:T(1,128)S(1)}, u32[]{:S(2)}, u32[]{:S(2)}) collective-permute-start(f32[4,1,1024]{2,1,0:T(1,128)S(1)} %slice_bitcast_fusion.28), channel_id=1, source_target_pairs={{0,4},{4,8},{8,12},{12,16},{16,20},{20,24},{24,28},{28,32},{32,36}... | collective-permute-start | bytes 49160 | tf_op jit(solution)/shard_map/ppermute | solution.py:30
  166.1 7.5 %collective-permute-start.26 = (f32[4,8,1]{1,0,2:T(4,128)S(1)}, f32[4,8,1]{1,0,2:T(4,128)S(1)}, u32[]{:S(2)}, u32[]{:S(2)}) collective-permute-start(f32[4,8,1]{1,0,2:T(4,128)S(1)} %bitcast.171), channel_id=1, source_target_pairs={{0,1},{1,2},{2,3},{4,5},{5,6},{6,7},{8,9},{9,10},{10,11},{12,13},{... | collective-permute-start | bytes 392 | tf_op jit(solution)/shard_map/ppermute | solution.py:30
  173.7 0.7 collective-permute-done.26
  174.5 0.8 fusion.31
  (94 shorter events, 2.7 us)
Async XLA Ops:
  0.0 2.7 %copy-start = (bf16[2,16,8,512]{3,2,1,0:T(8,128)(2,1)S(1)}, bf16[2,16,8,512]{3,2,1,0:T(8,128)(2,1)}, u32[]{:S(2)}) copy-start(bf16[2,16,8,512]{3,2,1,0:T(8,128)(2,1)} %param.7) | copy-start | bytes 786436
  22.4 23.8 %copy-start.1 = (f32[4,8,1024]{2,1,0:T(8,128)S(1)}, f32[4,8,1024]{2,1,0:T(8,128)}, u32[]{:S(2)}) copy-start(f32[4,8,1024]{2,1,0:T(8,128)} %param.13) | copy-start | bytes 393220
  22.4 23.8 %copy-start.2 = (f32[4,8,1024]{2,1,0:T(8,128)S(1)}, f32[4,8,1024]{2,1,0:T(8,128)}, u32[]{:S(2)}) copy-start(f32[4,8,1024]{2,1,0:T(8,128)} %param.12) | copy-start | bytes 393220
  24.0 21.3 %all-to-all-start = ((f32[4,4,8,1024]{3,2,1,0:T(8,128)}), f32[4,4,8,1024]{3,2,1,0:T(8,128)S(1)}, u32[]{:S(2)}, u32[]{:S(2)}) async-start(f32[4,4,8,1024]{3,2,1,0:T(8,128)} %bitcast.6), calls=%async_computation | async-start | bytes 1048576 | tf_op jit(solution)/shard_map/all_to_all | solution.py:23
  28.2 18.0 %collective-permute-start = (f32[1,8,1024]{2,1,0:T(8,128)S(1)}, f32[1,8,1024]{2,1,0:T(8,128)S(1)}, u32[]{:S(2)}, u32[]{:S(2)}) collective-permute-start(f32[1,8,1024]{2,1,0:T(8,128)S(1)} %squeeze.120), channel_id=1, source_target_pairs={{0,128},{128,256},{256,384},{1,129},{129,257},{257,385},{2,130},{1... | collective-permute-start | bytes 98312 | tf_op jit(solution)/shard_map/ppermute | solution.py:30
  31.6 14.6 %collective-permute-start.1 = (f32[4,1,1024]{2,1,0:T(1,128)S(1)}, f32[4,1,1024]{2,1,0:T(1,128)S(1)}, u32[]{:S(2)}, u32[]{:S(2)}) collective-permute-start(f32[4,1,1024]{2,1,0:T(1,128)S(1)} %squeeze.121), channel_id=1, source_target_pairs={{0,4},{4,8},{8,12},{12,16},{16,20},{20,24},{24,28},{28,32},{32,36}... | collective-permute-start | bytes 49160 | tf_op jit(solution)/shard_map/ppermute | solution.py:30
  36.5 9.7 %collective-permute-start.2 = (f32[4,8,1]{2,1,0:T(8,128)S(1)}, f32[4,8,1]{2,1,0:T(8,128)S(1)}, u32[]{:S(2)}, u32[]{:S(2)}) collective-permute-start(f32[4,8,1]{2,1,0:T(8,128)S(1)} %squeeze.122), channel_id=1, source_target_pairs={{0,1},{1,2},{2,3},{4,5},{5,6},{6,7},{8,9},{9,10},{10,11},{12,13},{... | collective-permute-start | bytes 392 | tf_op jit(solution)/shard_map/ppermute | solution.py:30
  46.3 12.6 %collective-permute-start.3 = (f32[1,8,1024]{2,1,0:T(8,128)S(1)}, f32[1,8,1024]{2,1,0:T(8,128)S(1)}, u32[]{:S(2)}, u32[]{:S(2)}) collective-permute-start(f32[1,8,1024]{2,1,0:T(8,128)S(1)} %slice.267), channel_id=1, source_target_pairs={{128,0},{256,128},{384,256},{129,1},{257,129},{385,257},{130,2},{2... | collective-permute-start | bytes 98312 | tf_op jit(solution)/shard_map/ppermute | solution.py:30
  47.6 11.3 %collective-permute-start.4 = (f32[4,1,1024]{2,1,0:T(1,128)S(1)}, f32[4,1,1024]{2,1,0:T(1,128)S(1)}, u32[]{:S(2)}, u32[]{:S(2)}) collective-permute-start(f32[4,1,1024]{2,1,0:T(1,128)S(1)} %slice.269), channel_id=1, source_target_pairs={{4,0},{8,4},{12,8},{16,12},{20,16},{24,20},{28,24},{32,28},{36,32}... | collective-permute-start | bytes 49160 | tf_op jit(solution)/shard_map/ppermute | solution.py:30
  49.6 9.3 %collective-permute-start.5 = (f32[4,8,1]{2,1,0:T(8,128)S(1)}, f32[4,8,1]{2,1,0:T(8,128)S(1)}, u32[]{:S(2)}, u32[]{:S(2)}) collective-permute-start(f32[4,8,1]{2,1,0:T(8,128)S(1)} %slice.271), channel_id=1, source_target_pairs={{1,0},{2,1},{3,2},{5,4},{6,5},{7,6},{9,8},{10,9},{11,10},{13,12},{... | collective-permute-start | bytes 392 | tf_op jit(solution)/shard_map/ppermute | solution.py:30
  59.4 19.5 %collective-permute-start.6 = (f32[1,8,1024]{2,1,0:T(8,128)S(1)}, f32[1,8,1024]{2,1,0:T(8,128)S(1)}, u32[]{:S(2)}, u32[]{:S(2)}) collective-permute-start(f32[1,8,1024]{2,1,0:T(8,128)S(1)} %slice_bitcast_fusion.27), channel_id=1, source_target_pairs={{0,128},{128,256},{256,384},{1,129},{129,257},{257,385},{2,130},{1... | collective-permute-start | bytes 98312 | tf_op jit(solution)/shard_map/ppermute | solution.py:30
  63.6 15.2 %collective-permute-start.7 = (f32[4,1,1024]{2,1,0:T(1,128)S(1)}, f32[4,1,1024]{2,1,0:T(1,128)S(1)}, u32[]{:S(2)}, u32[]{:S(2)}) collective-permute-start(f32[4,1,1024]{2,1,0:T(1,128)S(1)} %slice_bitcast_fusion.31), channel_id=1, source_target_pairs={{0,4},{4,8},{8,12},{12,16},{16,20},{20,24},{24,28},{28,32},{32,36}... | collective-permute-start | bytes 49160 | tf_op jit(solution)/shard_map/ppermute | solution.py:30
  70.1 8.6 %collective-permute-start.8 = (f32[4,8,1]{1,0,2:T(4,128)S(1)}, f32[4,8,1]{1,0,2:T(4,128)S(1)}, u32[]{:S(2)}, u32[]{:S(2)}) collective-permute-start(f32[4,8,1]{1,0,2:T(4,128)S(1)} %bitcast.168), channel_id=1, source_target_pairs={{0,1},{1,2},{2,3},{4,5},{5,6},{6,7},{8,9},{9,10},{10,11},{12,13},{... | collective-permute-start | bytes 392 | tf_op jit(solution)/shard_map/ppermute | solution.py:30
  78.9 12.3 %collective-permute-start.9 = (f32[1,8,1024]{2,1,0:T(8,128)S(1)}, f32[1,8,1024]{2,1,0:T(8,128)S(1)}, u32[]{:S(2)}, u32[]{:S(2)}) collective-permute-start(f32[1,8,1024]{2,1,0:T(8,128)S(1)} %slice.282), channel_id=1, source_target_pairs={{128,0},{256,128},{384,256},{129,1},{257,129},{385,257},{130,2},{2... | collective-permute-start | bytes 98312 | tf_op jit(solution)/shard_map/ppermute | solution.py:30
  80.3 10.9 %collective-permute-start.10 = (f32[4,1,1024]{2,1,0:T(1,128)S(1)}, f32[4,1,1024]{2,1,0:T(1,128)S(1)}, u32[]{:S(2)}, u32[]{:S(2)}) collective-permute-start(f32[4,1,1024]{2,1,0:T(1,128)S(1)} %slice.284), channel_id=1, source_target_pairs={{4,0},{8,4},{12,8},{16,12},{20,16},{24,20},{28,24},{32,28},{36,32}... | collective-permute-start | bytes 49160 | tf_op jit(solution)/shard_map/ppermute | solution.py:30
  82.2 9.0 %collective-permute-start.11 = (f32[4,8,1]{2,1,0:T(8,128)S(1)}, f32[4,8,1]{2,1,0:T(8,128)S(1)}, u32[]{:S(2)}, u32[]{:S(2)}) collective-permute-start(f32[4,8,1]{2,1,0:T(8,128)S(1)} %slice.286), channel_id=1, source_target_pairs={{1,0},{2,1},{3,2},{5,4},{6,5},{7,6},{9,8},{10,9},{11,10},{13,12},{... | collective-permute-start | bytes 392 | tf_op jit(solution)/shard_map/ppermute | solution.py:30
  91.7 19.0 %collective-permute-start.12 = (f32[1,8,1024]{2,1,0:T(8,128)S(1)}, f32[1,8,1024]{2,1,0:T(8,128)S(1)}, u32[]{:S(2)}, u32[]{:S(2)}) collective-permute-start(f32[1,8,1024]{2,1,0:T(8,128)S(1)} %slice_bitcast_fusion.26), channel_id=1, source_target_pairs={{0,128},{128,256},{256,384},{1,129},{129,257},{257,385},{2,130},{1... | collective-permute-start | bytes 98312 | tf_op jit(solution)/shard_map/ppermute | solution.py:30
  95.7 15.0 %collective-permute-start.13 = (f32[4,1,1024]{2,1,0:T(1,128)S(1)}, f32[4,1,1024]{2,1,0:T(1,128)S(1)}, u32[]{:S(2)}, u32[]{:S(2)}) collective-permute-start(f32[4,1,1024]{2,1,0:T(1,128)S(1)} %slice_bitcast_fusion.30), channel_id=1, source_target_pairs={{0,4},{4,8},{8,12},{12,16},{16,20},{20,24},{24,28},{28,32},{32,36}... | collective-permute-start | bytes 49160 | tf_op jit(solution)/shard_map/ppermute | solution.py:30
  102.3 8.3 %collective-permute-start.14 = (f32[4,8,1]{1,0,2:T(4,128)S(1)}, f32[4,8,1]{1,0,2:T(4,128)S(1)}, u32[]{:S(2)}, u32[]{:S(2)}) collective-permute-start(f32[4,8,1]{1,0,2:T(4,128)S(1)} %bitcast.169), channel_id=1, source_target_pairs={{0,1},{1,2},{2,3},{4,5},{5,6},{6,7},{8,9},{9,10},{10,11},{12,13},{... | collective-permute-start | bytes 392 | tf_op jit(solution)/shard_map/ppermute | solution.py:30
  110.8 11.9 %collective-permute-start.15 = (f32[1,8,1024]{2,1,0:T(8,128)S(1)}, f32[1,8,1024]{2,1,0:T(8,128)S(1)}, u32[]{:S(2)}, u32[]{:S(2)}) collective-permute-start(f32[1,8,1024]{2,1,0:T(8,128)S(1)} %slice.297), channel_id=1, source_target_pairs={{128,0},{256,128},{384,256},{129,1},{257,129},{385,257},{130,2},{2... | collective-permute-start | bytes 98312 | tf_op jit(solution)/shard_map/ppermute | solution.py:30
  112.1 10.6 %collective-permute-start.16 = (f32[4,1,1024]{2,1,0:T(1,128)S(1)}, f32[4,1,1024]{2,1,0:T(1,128)S(1)}, u32[]{:S(2)}, u32[]{:S(2)}) collective-permute-start(f32[4,1,1024]{2,1,0:T(1,128)S(1)} %slice.299), channel_id=1, source_target_pairs={{4,0},{8,4},{12,8},{16,12},{20,16},{24,20},{28,24},{32,28},{36,32}... | collective-permute-start | bytes 49160 | tf_op jit(solution)/shard_map/ppermute | solution.py:30
  114.1 8.6 %collective-permute-start.17 = (f32[4,8,1]{2,1,0:T(8,128)S(1)}, f32[4,8,1]{2,1,0:T(8,128)S(1)}, u32[]{:S(2)}, u32[]{:S(2)}) collective-permute-start(f32[4,8,1]{2,1,0:T(8,128)S(1)} %slice.301), channel_id=1, source_target_pairs={{1,0},{2,1},{3,2},{5,4},{6,5},{7,6},{9,8},{10,9},{11,10},{13,12},{... | collective-permute-start | bytes 392 | tf_op jit(solution)/shard_map/ppermute | solution.py:30
  123.3 19.3 %collective-permute-start.18 = (f32[1,8,1024]{2,1,0:T(8,128)S(1)}, f32[1,8,1024]{2,1,0:T(8,128)S(1)}, u32[]{:S(2)}, u32[]{:S(2)}) collective-permute-start(f32[1,8,1024]{2,1,0:T(8,128)S(1)} %slice_bitcast_fusion.25), channel_id=1, source_target_pairs={{0,128},{128,256},{256,384},{1,129},{129,257},{257,385},{2,130},{1... | collective-permute-start | bytes 98312 | tf_op jit(solution)/shard_map/ppermute | solution.py:30
  127.2 15.3 %collective-permute-start.19 = (f32[4,1,1024]{2,1,0:T(1,128)S(1)}, f32[4,1,1024]{2,1,0:T(1,128)S(1)}, u32[]{:S(2)}, u32[]{:S(2)}) collective-permute-start(f32[4,1,1024]{2,1,0:T(1,128)S(1)} %slice_bitcast_fusion.29), channel_id=1, source_target_pairs={{0,4},{4,8},{8,12},{12,16},{16,20},{20,24},{24,28},{28,32},{32,36}... | collective-permute-start | bytes 49160 | tf_op jit(solution)/shard_map/ppermute | solution.py:30
  134.2 8.2 %collective-permute-start.20 = (f32[4,8,1]{1,0,2:T(4,128)S(1)}, f32[4,8,1]{1,0,2:T(4,128)S(1)}, u32[]{:S(2)}, u32[]{:S(2)}) collective-permute-start(f32[4,8,1]{1,0,2:T(4,128)S(1)} %bitcast.170), channel_id=1, source_target_pairs={{0,1},{1,2},{2,3},{4,5},{5,6},{6,7},{8,9},{9,10},{10,11},{12,13},{... | collective-permute-start | bytes 392 | tf_op jit(solution)/shard_map/ppermute | solution.py:30
  142.7 11.9 %collective-permute-start.21 = (f32[1,8,1024]{2,1,0:T(8,128)S(1)}, f32[1,8,1024]{2,1,0:T(8,128)S(1)}, u32[]{:S(2)}, u32[]{:S(2)}) collective-permute-start(f32[1,8,1024]{2,1,0:T(8,128)S(1)} %slice.312), channel_id=1, source_target_pairs={{128,0},{256,128},{384,256},{129,1},{257,129},{385,257},{130,2},{2... | collective-permute-start | bytes 98312 | tf_op jit(solution)/shard_map/ppermute | solution.py:30
  144.0 10.6 %collective-permute-start.22 = (f32[4,1,1024]{2,1,0:T(1,128)S(1)}, f32[4,1,1024]{2,1,0:T(1,128)S(1)}, u32[]{:S(2)}, u32[]{:S(2)}) collective-permute-start(f32[4,1,1024]{2,1,0:T(1,128)S(1)} %slice.314), channel_id=1, source_target_pairs={{4,0},{8,4},{12,8},{16,12},{20,16},{24,20},{28,24},{32,28},{36,32}... | collective-permute-start | bytes 49160 | tf_op jit(solution)/shard_map/ppermute | solution.py:30
  145.9 8.6 %collective-permute-start.23 = (f32[4,8,1]{2,1,0:T(8,128)S(1)}, f32[4,8,1]{2,1,0:T(8,128)S(1)}, u32[]{:S(2)}, u32[]{:S(2)}) collective-permute-start(f32[4,8,1]{2,1,0:T(8,128)S(1)} %slice.316), channel_id=1, source_target_pairs={{1,0},{2,1},{3,2},{5,4},{6,5},{7,6},{9,8},{10,9},{11,10},{13,12},{... | collective-permute-start | bytes 392 | tf_op jit(solution)/shard_map/ppermute | solution.py:30
  155.2 19.3 %collective-permute-start.24 = (f32[1,8,1024]{2,1,0:T(8,128)S(1)}, f32[1,8,1024]{2,1,0:T(8,128)S(1)}, u32[]{:S(2)}, u32[]{:S(2)}) collective-permute-start(f32[1,8,1024]{2,1,0:T(8,128)S(1)} %slice_bitcast_fusion.24), channel_id=1, source_target_pairs={{0,128},{128,256},{256,384},{1,129},{129,257},{257,385},{2,130},{1... | collective-permute-start | bytes 98312 | tf_op jit(solution)/shard_map/ppermute | solution.py:30
  159.2 15.3 %collective-permute-start.25 = (f32[4,1,1024]{2,1,0:T(1,128)S(1)}, f32[4,1,1024]{2,1,0:T(1,128)S(1)}, u32[]{:S(2)}, u32[]{:S(2)}) collective-permute-start(f32[4,1,1024]{2,1,0:T(1,128)S(1)} %slice_bitcast_fusion.28), channel_id=1, source_target_pairs={{0,4},{4,8},{8,12},{12,16},{16,20},{20,24},{24,28},{28,32},{32,36}... | collective-permute-start | bytes 49160 | tf_op jit(solution)/shard_map/ppermute | solution.py:30
  166.1 8.2 %collective-permute-start.26 = (f32[4,8,1]{1,0,2:T(4,128)S(1)}, f32[4,8,1]{1,0,2:T(4,128)S(1)}, u32[]{:S(2)}, u32[]{:S(2)}) collective-permute-start(f32[4,8,1]{1,0,2:T(4,128)S(1)} %bitcast.171), channel_id=1, source_target_pairs={{0,1},{1,2},{2,3},{4,5},{5,6},{6,7},{8,9},{9,10},{10,11},{12,13},{... | collective-permute-start | bytes 392 | tf_op jit(solution)/shard_map/ppermute | solution.py:30
where the time goes:
time: 176 us; the launch traced here: 175 us
  starting transfers between devices  113 us (64%)
  waiting for transfers between devices  33.6 us (19%)
  other arithmetic  21.6 us (12%)
  matrix products  3.82 us (2%)
  local copies, waits for them, and re-layouts  2.66 us (2%)
    ppermute x27, starting transfers between devices, passed_along(): return lax.ppermute(block, axis, route)  109 us
    ppermute x27, waiting for transfers between devices, passed_along(): return lax.ppermute(block, axis, route)  33.6 us
    another operation x1, other arithmetic  17.4 us
    all_to_all x1, starting transfers between devices, summed_on_arrival(): lax.all_to_all(blocks, axis, split_axis=0, concat_axis=0, tiled=True)  4.19 us
  transfers between devices with their start and end apart: 28, of which 9 were waited for; matrix products, arithmetic and copies ran while one was open for 1% of the time, Pallas kernels for 0%

commit v1 on v0

v1 whole, which is shorter than its diff:
```python
import functools
import math

import jax
import jax.numpy as jnp
import numpy as np
from jax import lax
from jax.experimental import pallas as pl
from jax.experimental.pallas import tpu as pltpu
from jax.sharding import PartitionSpec as P

MESH = pl.DeviceIdType.MESH
TV_STEPS = 4
dual_step = 1.0 / 12.0
N_ANG = 4
HALO = 4


def wave_constants(length, columns):
    block = length // N_ANG
    width = columns // N_ANG
    freq = np.arange(length, dtype=np.int64)

    def rows(cells):
        phase = np.mod(freq[:, None] * cells[None, :], length)
        angle = phase.astype(np.float32) * np.float32(2.0 * math.pi / length)
        cos = np.cos(angle).reshape(N_ANG, block, -1)
        sin = np.sin(angle).reshape(N_ANG, block, -1)
        return np.concatenate([cos, -sin], axis=1).astype(jnp.bfloat16)

    main = rows(np.arange(columns)).reshape(N_ANG, 2 * block, N_ANG, width)
    edge_cells = np.zeros(128, np.int64)
    for b in range(N_ANG):
        edge_cells[8 * b : 8 * b + 4] = width * (b + 1) + np.arange(4)
        edge_cells[8 * b + 4 : 8 * b + 8] = width * b - 4 + np.arange(4)
    return np.ascontiguousarray(main.transpose(0, 2, 1, 3)), rows(edge_cells)


def body(
    sizes,
    data_hbm,
    offsets_hbm,
    views_hbm,
    taps_hbm,
    weights_hbm,
    volume_hbm,
    multiplier_hbm,
    wave_hbm,
    edge_hbm,
    out_ref,
    data,
    offsets,
    views,
    taps,
    weights,
    volume,
    multiplier,
    wave,
    edge,
    table,
    joined,
    vm_send,
    vm_tiles,
    vm_recv,
    vm_edge,
    part_send,
    part_recv,
    strip_send,
    strip_recv,
    turned,
    scaled,
    flows,
    masks,
    result,
    in_sem,
    vm_ssem,
    vm_rsem,
    ve_ssem,
    ve_rsem,
    pt_ssem,
    pt_rsem,
    st_ssem,
    st_rsem,
    hl_ssem,
    hl_rsem,
    out_ssem,
    out_rsem,
    own_sem,
):
    length, n_gy, n_gx = sizes
    block = length // N_ANG
    a, y, g = lax.axis_index("ang"), lax.axis_index("gy"), lax.axis_index("gx")
    peers = {d: lax.rem(a + d, N_ANG) for d in range(N_ANG)}

    barrier = pltpu.get_barrier_semaphore()

    def greet(where):
        pl.semaphore_signal(barrier, inc=1, device_id=where, device_id_type=MESH)

    for d in range(1, N_ANG):
        greet((peers[d], y, g))

    @pl.when(y > 0)
    def _():
        greet((a, y - 1, g))

    @pl.when(y < n_gy - 1)
    def _():
        greet((a, y + 1, g))

    @pl.when(jnp.logical_and(a == 0, g > 0))
    def _():
        for other in range(N_ANG):
            greet((other, y, g - 1))

    @pl.when(jnp.logical_and(a == N_ANG - 1, g < n_gx - 1))
    def _():
        for other in range(N_ANG):
            greet((other, y, g + 1))

    def fetch(src, dst, k):
        return pltpu.make_async_copy(src, dst, in_sem.at[k])

    small = [
        fetch(offsets_hbm, offsets, 0),
        fetch(views_hbm, views, 1),
        fetch(taps_hbm, taps, 2),
        fetch(weights_hbm, weights, 3),
        fetch(data_hbm, data, 4),
    ]
    fields = [fetch(volume_hbm, volume, 5), fetch(multiplier_hbm, multiplier, 6)]
    waves = {
        d: fetch(wave_hbm.at[a, peers[d]], wave.at[d], 7 + d) for d in range(N_ANG)
    }
    edges = fetch(edge_hbm.at[a], edge, 11)
    for copy in small + fields + [waves[2], waves[1], waves[3], edges, waves[0]]:
        copy.start()

    @pl.when(y == 0)
    def _():
        scaled[0:HALO] = jnp.zeros((HALO, 16, 384), jnp.float32)

    @pl.when(y == n_gy - 1)
    def _():
        scaled[8 + HALO :] = jnp.zeros((HALO, 16, 384), jnp.float32)

    lane = lax.broadcasted_iota(jnp.int32, (16, 384), 1)
    plane = lax.broadcasted_iota(jnp.int32, (16, 384), 0)
    first = jnp.logical_and(a == 0, g == 0)
    last = jnp.logical_and(a == N_ANG - 1, g == n_gx - 1)
    closed = jnp.logical_or(
        jnp.logical_and(lane == 383, first), jnp.logical_and(lane == 255, last)
    )
    masks[0] = jnp.where(closed, 0.0, dual_step)
    masks[1] = jnp.where(plane == 15, 0.0, dual_step)
    turned[...] = jnp.zeros((128, 128), jnp.float32)

    for copy in small:
        copy.wait()
    for h in range(11):
        table[h : h + 1, :] = weights[:, 128 * h : 128 * h + 128]
    tail = weights.shape[1] - 128
    table[11:12, :] = weights[:, tail : tail + 128]
    table[12:16, :] = jnp.zeros((4, 128), jnp.float32)
    full = table[...]
    high = full.astype(jnp.bfloat16)
    rest = full - high.astype(jnp.float32)
    mid = rest.astype(jnp.bfloat16)
    low = (rest - mid.astype(jnp.float32)).astype(jnp.bfloat16)
    ids = views[...]
    group = jnp.minimum(lax.shift_right_logical(ids, 7), 11)
    within = jnp.where(group == 11, ids - tail, ids - group * 128)
    hot = (lax.broadcasted_iota(jnp.int32, (128, 512), 0) == within).astype(jnp.float32)
    hot = hot.astype(jnp.bfloat16)
    picked = (
        jnp.dot(high, hot, preferred_element_type=jnp.float32)
        + jnp.dot(mid, hot, preferred_element_type=jnp.float32)
        + jnp.dot(low, hot, preferred_element_type=jnp.float32)
    )
    of_group = lax.broadcasted_iota(jnp.int32, (16, 512), 0) == group
    weight = jnp.sum(jnp.where(of_group, picked, 0.0), axis=0, keepdims=True)
    coefs = weight * taps[...]

    line_out = lax.broadcasted_iota(jnp.int32, (128, 128), 0)
    line_in = lax.broadcasted_iota(jnp.int32, (128, 128), 1)
    order = lax.rem(line_out, 16) * 8 + lax.div(line_out, 16)
    order = (line_in == order).astype(jnp.float32).astype(jnp.bfloat16)
    for c in range(2):
        data[128 * c : 128 * c + 128] = jnp.dot(
            order, data[128 * c : 128 * c + 128], preferred_element_type=jnp.float32
        ).astype(jnp.bfloat16)

    turn = g * (4 * 1024 // length)

    def grid_block(i, carry):
        base = pl.multiple_of(i * 256, 256)
        cell = lax.broadcasted_iota(jnp.int32, (256, 512), 0) + base
        away = cell - offsets[...]
        spread = jnp.zeros((256, 512), jnp.float32)
        for t in range(4):
            spread = jnp.where(away == t, coefs[t : t + 1], spread)
        gridded = lax.dot_general(
            data[...],
            spread.astype(jnp.bfloat16),
            (((1,), (1,)), ((), ())),
            preferred_element_type=jnp.float32,
        )
        re, im = gridded[:128], gridded[128:]
        quarter = jnp.bitwise_and(
            (lax.broadcasted_iota(jnp.int32, (1, 256), 1) + base) * turn, 3
        )
        odd = jnp.bitwise_and(quarter, 1) == 1
        re_sign = jnp.where(jnp.logical_or(quarter == 1, quarter == 2), -1.0, 1.0)
        im_sign = jnp.where(quarter >= 2, -1.0, 1.0)
        joined[:, pl.ds(base, 256)] = (jnp.where(odd, im, re) * re_sign).astype(jnp.bfloat16)
        joined[:, pl.ds(pl.multiple_of(base + block, 256), 256)] = (
            jnp.where(odd, re, im) * im_sign
        ).astype(jnp.bfloat16)
        return carry

    lax.fori_loop(0, block // 256, grid_block, 0)

    for copy in fields:
        copy.wait()
    low_lane = lax.broadcasted_iota(jnp.int32, (4, 8, 128), 2) < 64
    vm_send[...] = volume[...] + multiplier[...]
    for b in range(N_ANG):
        after = vm_send[:, :, pl.ds(256 * min(b + 1, 3), 128)]
        before = vm_send[:, :, pl.ds(256 * max(b, 1) - 128, 128)]
        vm_tiles[b] = jnp.where(low_lane, after, before)

    waves[2].wait()

    def transform(d):
        part_send[d] = jnp.dot(joined[...], wave[d], preferred_element_type=jnp.float32)

    transform(2)

    greeted = (
        N_ANG - 1
        + (y > 0).astype(jnp.int32)
        + (y < n_gy - 1).astype(jnp.int32)
        + (g > 0).astype(jnp.int32)
        + (g < n_gx - 1).astype(jnp.int32)
    )
    pl.semaphore_wait(barrier, greeted)

    def remote(src, dst, ssem, rsem, where):
        return pltpu.make_async_remote_copy(
            src_ref=src,
            dst_ref=dst,
            send_sem=ssem,
            recv_sem=rsem,
            device_id=where,
            device_id_type=MESH,
        )

    def part_copy(d, h):
        lines = pl.ds(64 * h, 64)
        return remote(
            part_send.at[d, lines],
            part_recv.at[d, lines],
            pt_ssem.at[d, h],
            pt_rsem.at[d, h],
            (peers[d], y, g),
        )

    def strip_copy(d):
        return remote(
            strip_send.at[peers[d]],
            strip_recv.at[d],
            st_ssem.at[d],
            st_rsem.at[d],
            (peers[d], y, g),
        )

    def vm_copies(d):
        mine = pl.ds(4 * a, 4)
        return [
            remote(
                vm_send.at[:, :, pl.ds(pl.multiple_of(256 * peers[d], 256), 256)],
                vm_recv.at[mine, :, pl.ds(0, 256)],
                vm_ssem.at[d, 0],
                vm_rsem.at[d, 0],
                (peers[d], y, g),
            ),
            remote(
                vm_tiles.at[peers[d]],
                vm_recv.at[mine, :, pl.ds(256, 128)],
                vm_ssem.at[d, 1],
                vm_rsem.at[d, 1],
                (peers[d], y, g),
            ),
        ]

    def vm_arrivals(d):
        theirs = pl.ds(4 * lax.rem(a + N_ANG - d, N_ANG), 4)
        return [
            remote(
                vm_send.at[:, :, pl.ds(0, 256)],
                vm_recv.at[theirs, :, pl.ds(0, 256)],
                vm_ssem.at[d, 0],
                vm_rsem.at[d, 0],
                (peers[d], y, g),
            ),
            remote(
                vm_tiles.at[0],
                vm_recv.at[theirs, :, pl.ds(256, 128)],
                vm_ssem.at[d, 1],
                vm_rsem.at[d, 1],
                (peers[d], y, g),
            ),
        ]

    def edge_copy(up, place, target):
        tile = 1024 - 128 if up else 0
        return remote(
            vm_send.at[:, :, pl.ds(tile, 128)],
            vm_edge.at[pl.ds(4 * place, 4)],
            ve_ssem.at[0 if up else 1],
            ve_rsem.at[place],
            target,
        )

    part_copy(2, 0).start()
    part_copy(2, 1).start()

    @pl.when(g < n_gx - 1)
    def _():
        edge_copy(True, a, (0, y, g + 1)).start()

    @pl.when(g > 0)
    def _():
        edge_copy(False, a, (N_ANG - 1, y, g - 1)).start()

    for d in (1, 3):
        waves[d].wait()
        transform(d)
        part_copy(d, 0).start()
        part_copy(d, 1).start()
    for d in (2, 1, 3):
        for copy in vm_copies(d):
            copy.start()
    edges.wait()
    strips = jnp.dot(joined[...], edge[...], preferred_element_type=jnp.float32)
    strips = jnp.transpose(strips)
    for b in range(N_ANG):
        strip_send[b] = strips[8 * b : 8 * b + 8]
    for d in (2, 1, 3):
        strip_copy(d).start()
    mine = pl.ds(4 * a, 4)
    vm_recv[mine, :, pl.ds(0, 256)] = vm_send[:, :, pl.ds(pl.multiple_of(256 * a, 256), 256)]
    vm_recv[mine, :, pl.ds(256, 128)] = vm_tiles[a]
    waves[0].wait()
    transform(0)

    for d in range(1, N_ANG):
        for copy in vm_arrivals(d):
            copy.wait_recv()
    takes_low = jnp.logical_and(a == 0, g > 0)
    takes_high = jnp.logical_and(a == N_ANG - 1, g < n_gx - 1)

    @pl.when(jnp.logical_or(takes_low, takes_high))
    def _():
        for place in range(N_ANG):
            edge_copy(True, place, (0, y, g)).wait_recv()
        at_low = lax.broadcasted_iota(jnp.int32, (16, 8, 128), 2) < 64
        swap = jnp.logical_xor(at_low, takes_low)
        vm_recv[:, :, pl.ds(256, 128)] = jnp.where(
            swap, vm_edge[...], vm_recv[:, :, pl.ds(256, 128)]
        )

    for half in range(2):
        for j in range(3):
            scaled[HALO : HALO + 8, pl.ds(8 * half, 8), pl.ds(128 * j, 128)] = jnp.swapaxes(
                vm_recv[pl.ds(8 * half, 8), :, pl.ds(128 * j, 128)], 0, 1
            )

    for d in range(1, N_ANG):
        strip_copy(d).wait_recv()
    strip = (strip_send[a] + strip_recv[1]) + (strip_recv[3] + strip_recv[2])
    sub = lax.broadcasted_iota(jnp.int32, (8, 128), 0)
    turned[0:8] = jnp.where(sub < 4, strip, 0.0)
    turned[120:128] = jnp.where(sub < 4, 0.0, strip)
    turned[...] = jnp.transpose(turned[...])
    unit = 2.0 * length**-0.5
    lower_dev, upper_dev = (a, y - 1, g), (a, y + 1, g)
    below = remote(
        scaled.at[pl.ds(HALO, HALO)],
        scaled.at[pl.ds(HALO + 8, HALO)],
        hl_ssem.at[0],
        hl_rsem.at[0],
        lower_dev,
    )
    above = remote(
        scaled.at[pl.ds(8, HALO)],
        scaled.at[pl.ds(0, HALO)],
        hl_ssem.at[1],
        hl_rsem.at[1],
        upper_dev,
    )
    for h in range(2):
        for d in range(1, N_ANG):
            part_copy(d, h).wait_recv()

        def settle(i, carry):
            lines = pl.ds(pl.multiple_of(16 * i, 16), 16)
            total = (part_send[0, lines] + part_recv[1, lines]) + (
                part_recv[3, lines] + part_recv[2, lines]
            )
            both = jnp.concatenate([total, turned[lines]], axis=1)
            own = scaled[HALO + i]
            scaled[HALO + i] = (own + own) - unit * both
            return carry

        lax.fori_loop(4 * h, 4 * h + 4, settle, 0)
        if h == 0:

            @pl.when(y > 0)
            def _():
                below.start()

        else:

            @pl.when(y < n_gy - 1)
            def _():
                above.start()

    top_row = 8 * y - HALO
    end_row = 8 * n_gy - 1

    def divergence(k, r):
        q0, q1, q2 = (flows[k, c, r] for c in range(3))
        below_plane = jnp.where(plane == 0, 0.0, pltpu.roll(q0, 1, 0))
        return (
            (q0 - below_plane) + (q1 - flows[k, 1, r - 1]) + (q2 - pltpu.roll(q2, 1, 1))
        )

    def target(k, r):
        if k == 0:
            return -scaled[r]
        return divergence(k - 1, r) - scaled[r]

    def sweep(k, start, count):
        def row(i, here):
            r = start + i
            up = target(k, r + 1)
            row_id = top_row + r
            closed_row = jnp.logical_or(row_id == -1, row_id == end_row)
            step_row = jnp.where(closed_row, 0.0, dual_step)
            g0 = (pltpu.roll(here, 15, 0) - here) * masks[1]
            g1 = (up - here) * step_row
            g2 = (pltpu.roll(here, 383, 1) - here) * masks[0]
            norm = jnp.sqrt((g0 * g0 + g1 * g1) + g2 * g2)
            scale = 1.0 / (1.0 + norm)
            for c, slope in enumerate((g0, g1, g2)):
                if k > 0:
                    slope = flows[k - 1, c, r] + slope
                flows[k, c, r] = slope * scale
            return up

        lax.fori_loop(0, count, row, target(k, start))

    for k in range(TV_STEPS):
        sweep(k, 4 + k, 7 - 2 * k)

    @pl.when(y > 0)
    def _():
        above.wait_recv()

    for k in range(TV_STEPS):
        sweep(k, k, 4)

    @pl.when(y < n_gy - 1)
    def _():
        below.wait_recv()

    for k in range(TV_STEPS):
        sweep(k, 11 - k, 4)

    def finish(i, carry):
        r = HALO + i
        scaled[r] = 0.5 * (scaled[r] - divergence(TV_STEPS - 1, r))
        return carry

    @pl.when(y > 0)
    def _():
        below.wait_send()

    @pl.when(y < n_gy - 1)
    def _():
        above.wait_send()

    lax.fori_loop(0, 8, finish, 0)
    for half in range(2):
        for j in range(2):
            result[pl.ds(8 * half, 8), :, pl.ds(128 * j, 128)] = jnp.swapaxes(
                scaled[HALO : HALO + 8, pl.ds(8 * half, 8), pl.ds(128 * j, 128)], 0, 1
            )

    def out_copy(d, column):
        return remote(
            result.at[pl.ds(4 * peers[d], 4)],
            out_ref.at[:, :, pl.ds(pl.multiple_of(256 * column, 256), 256)],
            out_ssem.at[d],
            out_rsem.at[d],
            (peers[d], y, g),
        )

    for d in (2, 1, 3):
        out_copy(d, a).start()
    own = pltpu.make_async_copy(
        result.at[pl.ds(4 * a, 4)],
        out_ref.at[:, :, pl.ds(pl.multiple_of(256 * a, 256), 256)],
        own_sem,
    )
    own.start()
    for d in range(1, N_ANG):
        part_copy(d, 0).wait_send()
        part_copy(d, 1).wait_send()
        strip_copy(d).wait_send()
        for copy in vm_copies(d):
            copy.wait_send()

    @pl.when(g < n_gx - 1)
    def _():
        edge_copy(True, a, (0, y, g)).wait_send()

    @pl.when(g > 0)
    def _():
        edge_copy(False, a, (0, y, g)).wait_send()

    own.wait()
    for d in range(1, N_ANG):
        out_copy(d, a).wait_send()
        out_copy(d, lax.rem(a + N_ANG - d, N_ANG)).wait_recv()


def per_device(sizes, spectrum_data, offsets, view_index, kernel, view_weight, volume, multiplier):
    length = sizes[0]
    columns = volume.shape[2]
    samples = offsets.shape[0]
    lines = 16 * 8
    main, edge = wave_constants(length, columns)
    block = length // N_ANG
    f32, bf16, i32 = jnp.float32, jnp.bfloat16, jnp.int32
    dma = pltpu.SemaphoreType.DMA
    views = view_weight.shape[0]
    scratch = [
        pltpu.VMEM((2 * lines, samples), bf16),
        pltpu.VMEM((1, samples), i32),
        pltpu.VMEM((1, samples), i32),
        pltpu.VMEM((4, samples), f32),
        pltpu.VMEM((1, views), f32),
        pltpu.VMEM((4, 8, columns), f32),
        pltpu.VMEM((4, 8, columns), f32),
        pltpu.VMEM((N_ANG, 2 * block, 256), bf16),
        pltpu.VMEM((2 * block, 128), bf16),
        pltpu.VMEM((16, 128), f32),
        pltpu.VMEM((lines, 2 * block), bf16),
        pltpu.VMEM((4, 8, columns), f32),
        pltpu.VMEM((N_ANG, 4, 8, 128), f32),
        pltpu.VMEM((16, 8, 384), f32),
        pltpu.VMEM((16, 8, 128), f32),
        pltpu.VMEM((N_ANG, lines, 256), f32),
        pltpu.VMEM((N_ANG, lines, 256), f32),
        pltpu.VMEM((N_ANG, 8, 128), f32),
        pltpu.VMEM((N_ANG, 8, 128), f32),
        pltpu.VMEM((128, 128), f32),
        pltpu.VMEM((16, 16, 384), f32),
        pltpu.VMEM((TV_STEPS, 3, 16, 16, 384), f32),
        pltpu.VMEM((2, 16, 384), f32),
        pltpu.VMEM((16, 8, 256), f32),
        dma((12,)),
        dma((N_ANG, 2)),
        dma((N_ANG, 2)),
        dma((2,)),
        dma((N_ANG,)),
        dma((N_ANG, 2)),
        dma((N_ANG, 2)),
        dma((N_ANG,)),
        dma((N_ANG,)),
        dma((2,)),
        dma((2,)),
        dma((N_ANG,)),
        dma((N_ANG,)),
        dma,
    ]
    return pl.pallas_call(
        functools.partial(body, sizes),
        name="laminography",
        out_shape=jax.ShapeDtypeStruct(volume.shape, f32),
        in_specs=[pl.BlockSpec(memory_space=pl.ANY)] * 9,
        out_specs=pl.BlockSpec(memory_space=pl.ANY),
        scratch_shapes=scratch,
        compiler_params=pltpu.CompilerParams(
            collective_id=0, has_side_effects=True, vmem_limit_bytes=60 << 20
        ),
    )(
        spectrum_data.reshape(2 * lines, samples),
        offsets.reshape(1, samples),
        view_index.reshape(1, samples),
        kernel,
        view_weight.reshape(1, views),
        volume,
        multiplier,
        jnp.asarray(main),
        jnp.asarray(edge),
    )


def solution(mesh):
    placed = (
        P(None, None, "gy", "ang"),
        P("ang"),
        P("ang"),
        P(None, "ang"),
        P(),
        P("ang", "gy", "gx"),
        P("ang", "gy", "gx"),
    )
    sizes = (1024 * mesh.shape["gx"], mesh.shape["gy"], mesh.shape["gx"])
    return jax.shard_map(
        functools.partial(per_device, sizes),
        mesh=mesh,
        in_specs=placed,
        out_specs=P("ang", "gy", "gx"),
        check_vma=False,
    )
```

time: 176 us -> 35.5 us (0.20)
  the two profiles are of different devices: /device:TPU:7 before, /device:TPU:160 now
where the time goes in v1:
time: 35.5 us; the launch traced here: 35.3 us
  Pallas kernels  32.4 us (91%)
  local copies, waits for them, and re-layouts  2.86 us (8%)
    pallas_call x1, Pallas kernels, per_device(): pl.pallas_call(functools.partial(body, sizes), name='laminography', out_s...  32.4 us
    unnamed x1, local copies, waits for them, and re-layouts  1.57 us
    reshape x1, local copies, waits for them, and re-layouts, per_device(): view_weight.reshape(1, views)  1.29 us

profile of v1, /device:TPU:160, one launch (start us, length us, event | category | flops | bytes accessed | tf_op | source)
XLA Modules:
  0.0 35.3 jit_solution(9254739832761337474)
XLA Ops:
  0.0 1.3 %reshape.15.weights_hbm = f32[1,1500]{1,0:T(1,128)} reshape(f32[1500]{0:T(1024)} %param.13) | data formatting | bytes 12000 | tf_op jit(solution)/shard_map/reshape | solution.py:604
  1.3 32.4 %laminography.1 = f32[4,8,1024]{2,1,0:T(8,128)} custom-call(bf16[256,512]{1,0:T(8,128)(2,1)} %bitcast.3, s32[1,512]{1,0:T(1,128)} %bitcast.4, s32[1,512]{1,0:T(1,128)} %bitcast.5, f32[4,512]{1,0:T(4,128)} %taps_hbm.1, f32[1,1500]{1,0:T(1,128)} %reshape.15.weights_hbm, f32[4,8,1024]{2,1,0:T(8,128)} %volume_hbm.1, f32[4,8,1024]{2,1,0:T(8,128)} %multiplier_hbm.1, ...), custom_call_target="tpu_custom_call" | custom-call | tf_op jit(solution)/shard_map/laminography/pallas_call | solution.py:589
  33.7 1.6 %copy.11 = f32[4,8,1024]{2,1,0:T(8,128)} copy(f32[4,8,1024]{2,1,0:T(8,128)} %laminography.1) | data formatting | bytes 262144

commit v2 on v1

--- a/solution.py
+++ b/solution.py
@@ -59,10 +59,10 @@
     edge,
     table,
     joined,
-    vm_send,
-    vm_tiles,
-    vm_recv,
-    vm_edge,
+    field,
+    pieces,
+    field_edge,
+    extra,
     part_send,
     part_recv,
     strip_send,
@@ -70,11 +70,9 @@
     turned,
     scaled,
     flows,
-    masks,
+    done,
     result,
     in_sem,
-    vm_ssem,
-    vm_rsem,
     ve_ssem,
     ve_rsem,
     pt_ssem,
@@ -144,23 +142,16 @@
     def _():
         scaled[8 + HALO :] = jnp.zeros((HALO, 16, 384), jnp.float32)
 
-    lane = lax.broadcasted_iota(jnp.int32, (16, 384), 1)
-    plane = lax.broadcasted_iota(jnp.int32, (16, 384), 0)
-    first = jnp.logical_and(a == 0, g == 0)
-    last = jnp.logical_and(a == N_ANG - 1, g == n_gx - 1)
-    closed = jnp.logical_or(
-        jnp.logical_and(lane == 383, first), jnp.logical_and(lane == 255, last)
-    )
-    masks[0] = jnp.where(closed, 0.0, dual_step)
-    masks[1] = jnp.where(plane == 15, 0.0, dual_step)
     turned[...] = jnp.zeros((128, 128), jnp.float32)
+    extra[...] = jnp.zeros((8, 16, 128), jnp.float32)
+    pieces[96:128] = jnp.zeros((32, 1024), jnp.bfloat16)
 
     for copy in small:
         copy.wait()
     for h in range(11):
-        table[h : h + 1, :] = weights[:, 128 * h : 128 * h + 128]
-    tail = weights.shape[1] - 128
-    table[11:12, :] = weights[:, tail : tail + 128]
+        table[h : h + 1, :] = weights[pl.ds(128 * h, 128)].reshape(1, 128)
+    tail = weights.shape[0] - 128
+    table[11:12, :] = weights[pl.ds(tail, 128)].reshape(1, 128)
     table[12:16, :] = jnp.zeros((4, 128), jnp.float32)
     full = table[...]
     high = full.astype(jnp.bfloat16)
@@ -191,11 +182,10 @@
         ).astype(jnp.bfloat16)
 
     turn = g * (4 * 1024 // length)
-
-    def grid_block(i, carry):
-        base = pl.multiple_of(i * 256, 256)
-        cell = lax.broadcasted_iota(jnp.int32, (256, 512), 0) + base
-        away = cell - offsets[...]
+    firsts = offsets[...]
+    for i in range(block // 256):
+        base = 256 * i
+        away = lax.broadcasted_iota(jnp.int32, (256, 512), 0) + base - firsts
         spread = jnp.zeros((256, 512), jnp.float32)
         for t in range(4):
             spread = jnp.where(away == t, coefs[t : t + 1], spread)
@@ -212,30 +202,34 @@
         odd = jnp.bitwise_and(quarter, 1) == 1
         re_sign = jnp.where(jnp.logical_or(quarter == 1, quarter == 2), -1.0, 1.0)
         im_sign = jnp.where(quarter >= 2, -1.0, 1.0)
-        joined[:, pl.ds(base, 256)] = (jnp.where(odd, im, re) * re_sign).astype(jnp.bfloat16)
-        joined[:, pl.ds(pl.multiple_of(base + block, 256), 256)] = (
+        joined[:, base : base + 256] = (jnp.where(odd, im, re) * re_sign).astype(jnp.bfloat16)
+        joined[:, base + block : base + block + 256] = (
             jnp.where(odd, re, im) * im_sign
         ).astype(jnp.bfloat16)
-        return carry
-
-    lax.fori_loop(0, block // 256, grid_block, 0)
 
     for copy in fields:
         copy.wait()
-    low_lane = lax.broadcasted_iota(jnp.int32, (4, 8, 128), 2) < 64
-    vm_send[...] = volume[...] + multiplier[...]
-    for b in range(N_ANG):
-        after = vm_send[:, :, pl.ds(256 * min(b + 1, 3), 128)]
-        before = vm_send[:, :, pl.ds(256 * max(b, 1) - 128, 128)]
-        vm_tiles[b] = jnp.where(low_lane, after, before)
+    field[...] = volume[...] + multiplier[...]
+    rest = (-(length**0.5)) * field[...].reshape(32, 1024)
+    for j in range(3):
+        piece = rest.astype(jnp.bfloat16)
+        pieces[32 * j : 32 * j + 32] = piece
+        rest = rest - piece.astype(jnp.float32)
+    held_line = lax.broadcasted_iota(jnp.int32, (128, 128), 1)
+    line = lax.broadcasted_iota(jnp.int32, (128, 128), 0)
+    held = jnp.bitwise_and(held_line, 31)
+    home = lax.rem(held, 8) * 16 + lax.div(held, 8) + 4 * a
+    own_lines = jnp.where(jnp.logical_and(line == home, held_line < 96), 1.0, 0.0)
+    own_lines = own_lines.astype(jnp.bfloat16)
+
+    def transform(d):
+        cells = pl.ds(pl.multiple_of(256 * peers[d], 256), 256)
+        part_send[d] = jnp.dot(
+            joined[...], wave[d], preferred_element_type=jnp.float32
+        ) + jnp.dot(own_lines, pieces[:, cells], preferred_element_type=jnp.float32)
 
     waves[2].wait()
-
-    def transform(d):
-        part_send[d] = jnp.dot(joined[...], wave[d], preferred_element_type=jnp.float32)
-
     transform(2)
-
     greeted = (
         N_ANG - 1
         + (y > 0).astype(jnp.int32)
@@ -274,89 +268,50 @@
             (peers[d], y, g),
         )
 
-    def vm_copies(d):
-        mine = pl.ds(4 * a, 4)
-        return [
-            remote(
-                vm_send.at[:, :, pl.ds(pl.multiple_of(256 * peers[d], 256), 256)],
-                vm_recv.at[mine, :, pl.ds(0, 256)],
-                vm_ssem.at[d, 0],
-                vm_rsem.at[d, 0],
-                (peers[d], y, g),
-            ),
-            remote(
-                vm_tiles.at[peers[d]],
-                vm_recv.at[mine, :, pl.ds(256, 128)],
-                vm_ssem.at[d, 1],
-                vm_rsem.at[d, 1],
-                (peers[d], y, g),
-            ),
-        ]
-
-    def vm_arrivals(d):
-        theirs = pl.ds(4 * lax.rem(a + N_ANG - d, N_ANG), 4)
-        return [
-            remote(
-                vm_send.at[:, :, pl.ds(0, 256)],
-                vm_recv.at[theirs, :, pl.ds(0, 256)],
-                vm_ssem.at[d, 0],
-                vm_rsem.at[d, 0],
-                (peers[d], y, g),
-            ),
-            remote(
-                vm_tiles.at[0],
-                vm_recv.at[theirs, :, pl.ds(256, 128)],
-                vm_ssem.at[d, 1],
-                vm_rsem.at[d, 1],
-                (peers[d], y, g),
-            ),
-        ]
-
     def edge_copy(up, place, target):
         tile = 1024 - 128 if up else 0
         return remote(
-            vm_send.at[:, :, pl.ds(tile, 128)],
-            vm_edge.at[pl.ds(4 * place, 4)],
+            field.at[:, :, pl.ds(tile, 128)],
+            field_edge.at[pl.ds(4 * place, 4)],
             ve_ssem.at[0 if up else 1],
             ve_rsem.at[place],
             target,
         )
 
+    @pl.when(g < n_gx - 1)
+    def _():
+        edge_copy(True, a, (0, y, g + 1)).start()
+
+    @pl.when(g > 0)
+    def _():
+        edge_copy(False, a, (N_ANG - 1, y, g - 1)).start()
+
     part_copy(2, 0).start()
     part_copy(2, 1).start()
-
-    @pl.when(g < n_gx - 1)
-    def _():
-        edge_copy(True, a, (0, y, g + 1)).start()
-
-    @pl.when(g > 0)
-    def _():
-        edge_copy(False, a, (N_ANG - 1, y, g - 1)).start()
 
     for d in (1, 3):
         waves[d].wait()
         transform(d)
         part_copy(d, 0).start()
         part_copy(d, 1).start()
-    for d in (2, 1, 3):
-        for copy in vm_copies(d):
-            copy.start()
     edges.wait()
-    strips = jnp.dot(joined[...], edge[...], preferred_element_type=jnp.float32)
+    slot = lax.broadcasted_iota(jnp.int32, (1, 128), 1)
+    near = jnp.bitwise_and(slot, 7)
+    cell = 32 * (slot - near) + jnp.where(near < 4, 256 + near, near - 8)
+    chosen = lax.broadcasted_iota(jnp.int32, (1024, 128), 0) == cell
+    chosen = jnp.where(jnp.logical_and(chosen, slot < 32), 1.0, 0.0).astype(jnp.bfloat16)
+    near_pieces = jnp.dot(pieces[...], chosen, preferred_element_type=jnp.float32)
+    strips = jnp.dot(joined[...], edge[...], preferred_element_type=jnp.float32) + jnp.dot(
+        own_lines, near_pieces.astype(jnp.bfloat16), preferred_element_type=jnp.float32
+    )
     strips = jnp.transpose(strips)
     for b in range(N_ANG):
         strip_send[b] = strips[8 * b : 8 * b + 8]
     for d in (2, 1, 3):
         strip_copy(d).start()
-    mine = pl.ds(4 * a, 4)
-    vm_recv[mine, :, pl.ds(0, 256)] = vm_send[:, :, pl.ds(pl.multiple_of(256 * a, 256), 256)]
-    vm_recv[mine, :, pl.ds(256, 128)] = vm_tiles[a]
     waves[0].wait()
     transform(0)
 
-    for d in range(1, N_ANG):
-        for copy in vm_arrivals(d):
-            copy.wait_recv()
     takes_low = jnp.logical_and(a == 0, g > 0)
     takes_high = jnp.logical_and(a == N_ANG - 1, g < n_gx - 1)
 
@@ -365,15 +320,11 @@
         for place in range(N_ANG):
             edge_copy(True, place, (0, y, g)).wait_recv()
         at_low = lax.broadcasted_iota(jnp.int32, (16, 8, 128), 2) < 64
-        swap = jnp.logical_xor(at_low, takes_low)
-        vm_recv[:, :, pl.ds(256, 128)] = jnp.where(
-            swap, vm_edge[...], vm_recv[:, :, pl.ds(256, 128)]
-        )
-
-    for half in range(2):
-        for j in range(3):
-            scaled[HALO : HALO + 8, pl.ds(8 * half, 8), pl.ds(128 * j, 128)] = jnp.swapaxes(
-                vm_recv[pl.ds(8 * half, 8), :, pl.ds(128 * j, 128)], 0, 1
+        shown = jnp.logical_xor(at_low, takes_low)
+        field_edge[...] = jnp.where(shown, field_edge[...], 0.0)
+        for half in range(2):
+            extra[:, pl.ds(8 * half, 8), :] = jnp.swapaxes(
+                field_edge[pl.ds(8 * half, 8)], 0, 1
             )
 
     for d in range(1, N_ANG):
@@ -403,17 +354,14 @@
         for d in range(1, N_ANG):
             part_copy(d, h).wait_recv()
 
-        def settle(i, carry):
-            lines = pl.ds(pl.multiple_of(16 * i, 16), 16)
+        for i in range(4 * h, 4 * h + 4):
+            lines = slice(16 * i, 16 * i + 16)
             total = (part_send[0, lines] + part_recv[1, lines]) + (
                 part_recv[3, lines] + part_recv[2, lines]
             )
-            both = jnp.concatenate([total, turned[lines]], axis=1)
-            own = scaled[HALO + i]
-            scaled[HALO + i] = (own + own) - unit * both
-            return carry
-
-        lax.fori_loop(4 * h, 4 * h + 4, settle, 0)
+            beside = extra[i]
+            scaled[HALO + i, :, 0:256] = total * -unit
+            scaled[HALO + i, :, 256:384] = (beside + beside) - unit * turned[lines]
         if h == 0:
 
             @pl.when(y > 0)
@@ -426,12 +374,24 @@
             def _():
                 above.start()
 
-    top_row = 8 * y - HALO
-    end_row = 8 * n_gy - 1
+    lane = lax.broadcasted_iota(jnp.int32, (16, 384), 1)
+    plane = lax.broadcasted_iota(jnp.int32, (16, 384), 0)
+    first = jnp.logical_and(a == 0, g == 0)
+    last = jnp.logical_and(a == N_ANG - 1, g == n_gx - 1)
+    closed = jnp.logical_or(
+        jnp.logical_and(lane == 383, first), jnp.logical_and(lane == 255, last)
+    )
+    cell_step = jnp.where(closed, 0.0, dual_step)
+    plane_step = jnp.where(plane == 15, 0.0, dual_step)
+    lowest = plane == 0
+    row_steps = {
+        3: jnp.where(y == 0, 0.0, dual_step),
+        11: jnp.where(y == n_gy - 1, 0.0, dual_step),
+    }
 
     def divergence(k, r):
         q0, q1, q2 = (flows[k, c, r] for c in range(3))
-        below_plane = jnp.where(plane == 0, 0.0, pltpu.roll(q0, 1, 0))
+        below_plane = jnp.where(lowest, 0.0, pltpu.roll(q0, 1, 0))
         return (
             (q0 - below_plane) + (q1 - flows[k, 1, r - 1]) + (q2 - pltpu.roll(q2, 1, 1))
         )
@@ -441,61 +401,45 @@
             return -scaled[r]
         return divergence(k - 1, r) - scaled[r]
 
-    def sweep(k, start, count):
-        def row(i, here):
-            r = start + i
-            up = target(k, r + 1)
-            row_id = top_row + r
-            closed_row = jnp.logical_or(row_id == -1, row_id == end_row)
-            step_row = jnp.where(closed_row, 0.0, dual_step)
-            g0 = (pltpu.roll(here, 15, 0) - here) * masks[1]
-            g1 = (up - here) * step_row
-            g2 = (pltpu.roll(here, 383, 1) - here) * masks[0]
-            norm = jnp.sqrt((g0 * g0 + g1 * g1) + g2 * g2)
+    def sweep(k, rows):
+        targets = {}
+        for r in rows:
+            for near in (r, r + 1):
+                if near not in targets:
+                    targets[near] = target(k, near)
+            here = targets[r]
+            g0 = (pltpu.roll(here, 15, 0) - here) * plane_step
+            g1 = (targets[r + 1] - here) * row_steps.get(r, dual_step)
+            g2 = (pltpu.roll(here, 383, 1) - here) * cell_step
+            square = (g0 * g0 + g1 * g1) + g2 * g2
+            norm = square * lax.rsqrt(jnp.maximum(square, 1e-37))
             scale = 1.0 / (1.0 + norm)
             for c, slope in enumerate((g0, g1, g2)):
                 if k > 0:
                     slope = flows[k - 1, c, r] + slope
                 flows[k, c, r] = slope * scale
-            return up
-
-        lax.fori_loop(0, count, row, target(k, start))
 
     for k in range(TV_STEPS):
-        sweep(k, 4 + k, 7 - 2 * k)
+        sweep(k, range(4 + k, 11 - k))
 
     @pl.when(y > 0)
     def _():
         above.wait_recv()
 
+    @pl.when(y < n_gy - 1)
+    def _():
+        below.wait_recv()
+
     for k in range(TV_STEPS):
-        sweep(k, k, 4)
-
-    @pl.when(y < n_gy - 1)
-    def _():
-        below.wait_recv()
-
-    for k in range(TV_STEPS):
-        sweep(k, 11 - k, 4)
-
-    def finish(i, carry):
-        r = HALO + i
-        scaled[r] = 0.5 * (scaled[r] - divergence(TV_STEPS - 1, r))
-        return carry
-
-    @pl.when(y > 0)
-    def _():
-        below.wait_send()
-
-    @pl.when(y < n_gy - 1)
-    def _():
-        above.wait_send()
-
-    lax.fori_loop(0, 8, finish, 0)
+        pairs = zip(range(k, k + 4), range(11 - k, 15 - k))
+        sweep(k, [r for pair in pairs for r in pair])
+    for r in range(HALO, HALO + 8):
+        rest = 0.5 * (scaled[r] - divergence(TV_STEPS - 1, r))
+        done[r - HALO] = rest[:, 0:256]
     for half in range(2):
         for j in range(2):
             result[pl.ds(8 * half, 8), :, pl.ds(128 * j, 128)] = jnp.swapaxes(
-                scaled[HALO : HALO + 8, pl.ds(8 * half, 8), pl.ds(128 * j, 128)], 0, 1
+                done[:, pl.ds(8 * half, 8), pl.ds(128 * j, 128)], 0, 1
             )
 
     def out_copy(d, column):
@@ -519,8 +463,14 @@
         part_copy(d, 0).wait_send()
         part_copy(d, 1).wait_send()
         strip_copy(d).wait_send()
-        for copy in vm_copies(d):
-            copy.wait_send()
+
+    @pl.when(y > 0)
+    def _():
+        below.wait_send()
+
+    @pl.when(y < n_gy - 1)
+    def _():
+        above.wait_send()
 
     @pl.when(g < n_gx - 1)
     def _():
@@ -551,7 +501,7 @@
         pltpu.VMEM((1, samples), i32),
         pltpu.VMEM((1, samples), i32),
         pltpu.VMEM((4, samples), f32),
-        pltpu.VMEM((1, views), f32),
+        pltpu.VMEM((views,), f32),
         pltpu.VMEM((4, 8, columns), f32),
         pltpu.VMEM((4, 8, columns), f32),
         pltpu.VMEM((N_ANG, 2 * block, 256), bf16),
@@ -559,9 +509,9 @@
         pltpu.VMEM((16, 128), f32),
         pltpu.VMEM((lines, 2 * block), bf16),
         pltpu.VMEM((4, 8, columns), f32),
-        pltpu.VMEM((N_ANG, 4, 8, 128), f32),
-        pltpu.VMEM((16, 8, 384), f32),
+        pltpu.VMEM((128, columns), bf16),
         pltpu.VMEM((16, 8, 128), f32),
+        pltpu.VMEM((8, 16, 128), f32),
         pltpu.VMEM((N_ANG, lines, 256), f32),
         pltpu.VMEM((N_ANG, lines, 256), f32),
         pltpu.VMEM((N_ANG, 8, 128), f32),
@@ -569,11 +519,9 @@
         pltpu.VMEM((128, 128), f32),
         pltpu.VMEM((16, 16, 384), f32),
         pltpu.VMEM((TV_STEPS, 3, 16, 16, 384), f32),
-        pltpu.VMEM((2, 16, 384), f32),
+        pltpu.VMEM((8, 16, 256), f32),
         pltpu.VMEM((16, 8, 256), f32),
         dma((12,)),
-        dma((N_ANG, 2)),
-        dma((N_ANG, 2)),
         dma((2,)),
         dma((N_ANG,)),
         dma((N_ANG, 2)),
@@ -589,9 +537,9 @@
     return pl.pallas_call(
         functools.partial(body, sizes),
         name="laminography",
-        out_shape=jax.ShapeDtypeStruct(volume.shape, f32),
+        out_shape=pltpu.VMEM(volume.shape, f32),
         in_specs=[pl.BlockSpec(memory_space=pl.ANY)] * 9,
-        out_specs=pl.BlockSpec(memory_space=pl.ANY),
+        out_specs=pl.BlockSpec(memory_space=pltpu.VMEM),
         scratch_shapes=scratch,
         compiler_params=pltpu.CompilerParams(
             collective_id=0, has_side_effects=True, vmem_limit_bytes=60 << 20
@@ -601,7 +549,7 @@
         offsets.reshape(1, samples),
         view_index.reshape(1, samples),
         kernel,
-        view_weight.reshape(1, views),
+        view_weight,
         volume,
         multiplier,
         jnp.asarray(main),

time: 35.5 us -> 28.9 us (0.81)
  the two profiles are of different devices: /device:TPU:160 before, /device:TPU:1 now
where the time goes in v2:
time: 28.9 us; the launch traced here: 28.8 us
  Pallas kernels  28.1 us (97%)
  local copies, waits for them, and re-layouts  0.66 us (2%)
    pallas_call x1, Pallas kernels, per_device(): pl.pallas_call(functools.partial(body, sizes), name='laminography', out_s...  28.1 us
    unnamed x1, local copies, waits for them, and re-layouts  0.66 us

profile of v2, /device:TPU:1, one launch (start us, length us, event | category | flops | bytes accessed | tf_op | source)
XLA Modules:
  0.0 28.8 jit_solution(14676731306355084640)
XLA Ops:
  0.0 28.1 %laminography.1 = f32[4,8,1024]{2,1,0:T(8,128)S(1)} custom-call(bf16[256,512]{1,0:T(8,128)(2,1)} %bitcast.3, s32[1,512]{1,0:T(1,128)} %bitcast.4, s32[1,512]{1,0:T(1,128)} %bitcast.5, f32[4,512]{1,0:T(4,128)} %taps_hbm.1, f32[1500]{0:T(1024)} %weights_hbm.1, f32[4,8,1024]{2,1,0:T(8,128)} %volume_hbm.1, f32[4,8,1024]{2,1,0:T(8,128)} %multiplier_hbm.1, ...), custom_call_target="tpu_custom_call" | custom-call | tf_op jit(solution)/shard_map/laminography/pallas_call | solution.py:537
  28.1 0.7 %copy.11 = f32[4,8,1024]{2,1,0:T(8,128)} copy(f32[4,8,1024]{2,1,0:T(8,128)S(1)} %laminography.1) | data formatting | bytes 262144

commit v3 on v2

--- a/solution.py
+++ b/solution.py
@@ -84,12 +84,21 @@
     out_ssem,
     out_rsem,
     own_sem,
+    ready_left,
+    ready_right,
 ):
     length, n_gy, n_gx = sizes
     block = length // N_ANG
     a, y, g = lax.axis_index("ang"), lax.axis_index("gy"), lax.axis_index("gx")
     peers = {d: lax.rem(a + d, N_ANG) for d in range(N_ANG)}
 
+    middle = n_gx // 2
+    up_left = jnp.logical_and(g > 0, g < middle + 1)
+    down_left = g > middle
+    up_right = g < middle
+    down_right = jnp.logical_and(g > middle - 1, g < n_gx - 1)
+    answers_left = jnp.logical_and(a == 0, up_left)
+    answers_right = jnp.logical_and(a == N_ANG - 1, down_right)
     barrier = pltpu.get_barrier_semaphore()
 
     def greet(where):
@@ -106,12 +115,20 @@
     def _():
         greet((a, y + 1, g))
 
-    @pl.when(jnp.logical_and(a == 0, g > 0))
+    @pl.when(up_right)
+    def _():
+        greet((0, y, g + 1))
+
+    @pl.when(down_left)
+    def _():
+        greet((N_ANG - 1, y, g - 1))
+
+    @pl.when(jnp.logical_and(a == 0, down_left))
     def _():
         for other in range(N_ANG):
             greet((other, y, g - 1))
 
-    @pl.when(jnp.logical_and(a == N_ANG - 1, g < n_gx - 1))
+    @pl.when(jnp.logical_and(a == N_ANG - 1, up_right))
     def _():
         for other in range(N_ANG):
             greet((other, y, g + 1))
@@ -234,10 +251,25 @@
         N_ANG - 1
         + (y > 0).astype(jnp.int32)
         + (y < n_gy - 1).astype(jnp.int32)
-        + (g > 0).astype(jnp.int32)
-        + (g < n_gx - 1).astype(jnp.int32)
+        + up_left.astype(jnp.int32)
+        + down_right.astype(jnp.int32)
+        + N_ANG * answers_left.astype(jnp.int32)
+        + N_ANG * answers_right.astype(jnp.int32)
     )
     pl.semaphore_wait(barrier, greeted)
+
+    def answer(semaphore, where):
+        pl.semaphore_signal(semaphore, inc=1, device_id=where, device_id_type=MESH)
+
+    @pl.when(answers_left)
+    def _():
+        for other in range(N_ANG):
+            answer(ready_right, (other, y, g - 1))
+
+    @pl.when(answers_right)
+    def _():
+        for other in range(N_ANG):
+            answer(ready_left, (other, y, g + 1))
 
     def remote(src, dst, ssem, rsem, where):
         return pltpu.make_async_remote_copy(
@@ -278,13 +310,23 @@
             target,
         )
 
-    @pl.when(g < n_gx - 1)
+    @pl.when(down_right)
     def _():
         edge_copy(True, a, (0, y, g + 1)).start()
 
-    @pl.when(g > 0)
+    @pl.when(up_left)
     def _():
         edge_copy(False, a, (N_ANG - 1, y, g - 1)).start()
+
+    takes_low = jnp.logical_and(a == 0, g > 0)
+    takes_high = jnp.logical_and(a == N_ANG - 1, g < n_gx - 1)
+    takes = jnp.logical_or(takes_low, takes_high)
+
+    def send_answered(which):
+        @pl.when(jnp.logical_and(which, up_right))
+        def _():
+            pl.semaphore_wait(ready_right, 1)
+            edge_copy(True, a, (0, y, g + 1)).start()
 
     part_copy(2, 0).start()
     part_copy(2, 1).start()
@@ -312,10 +354,14 @@
     waves[0].wait()
     transform(0)
 
-    takes_low = jnp.logical_and(a == 0, g > 0)
-    takes_high = jnp.logical_and(a == N_ANG - 1, g < n_gx - 1)
-
-    @pl.when(jnp.logical_or(takes_low, takes_high))
+    @pl.when(down_left)
+    def _():
+        pl.semaphore_wait(ready_left, 1)
+        edge_copy(False, a, (N_ANG - 1, y, g - 1)).start()
+
+    send_answered(takes)
+
+    @pl.when(takes)
     def _():
         for place in range(N_ANG):
             edge_copy(True, place, (0, y, g)).wait_recv()
@@ -373,6 +419,8 @@
             @pl.when(y < n_gy - 1)
             def _():
                 above.start()
+
+    send_answered(jnp.logical_not(takes))
 
     lane = lax.broadcasted_iota(jnp.int32, (16, 384), 1)
     plane = lax.broadcasted_iota(jnp.int32, (16, 384), 0)
@@ -533,6 +581,8 @@
         dma((N_ANG,)),
         dma((N_ANG,)),
         dma,
+        pltpu.SemaphoreType.REGULAR,
+        pltpu.SemaphoreType.REGULAR,
     ]
     return pl.pallas_call(
         functools.partial(body, sizes),

time: 28.9 us -> 27.2 us (0.941)
  the two profiles are of different devices: /device:TPU:1 before, /device:TPU:360 now
where the time goes in v3:
time: 27.2 us; the launch traced here: 27.1 us
  Pallas kernels  26.4 us (97%)
  local copies, waits for them, and re-layouts  0.66 us (2%)
    pallas_call x1, Pallas kernels, per_device(): pl.pallas_call(functools.partial(body, sizes), name='laminography', out_s...  26.4 us
    unnamed x1, local copies, waits for them, and re-layouts  0.66 us

profile of v3, /device:TPU:360, one launch (start us, length us, event | category | flops | bytes accessed | tf_op | source)
XLA Modules:
  0.0 27.1 jit_solution(3787169258058938367)
XLA Ops:
  0.0 26.4 %laminography.1 = f32[4,8,1024]{2,1,0:T(8,128)S(1)} custom-call(bf16[256,512]{1,0:T(8,128)(2,1)} %bitcast.3, s32[1,512]{1,0:T(1,128)} %bitcast.4, s32[1,512]{1,0:T(1,128)} %bitcast.5, f32[4,512]{1,0:T(4,128)} %taps_hbm.1, f32[1500]{0:T(1024)} %weights_hbm.1, f32[4,8,1024]{2,1,0:T(8,128)} %volume_hbm.1, f32[4,8,1024]{2,1,0:T(8,128)} %multiplier_hbm.1, ...), custom_call_target="tpu_custom_call" | custom-call | tf_op jit(solution)/shard_map/laminography/pallas_call | solution.py:587
  26.5 0.7 %copy.11 = f32[4,8,1024]{2,1,0:T(8,128)} copy(f32[4,8,1024]{2,1,0:T(8,128)S(1)} %laminography.1) | data formatting | bytes 262144

commit v4 on v3

--- a/solution.py
+++ b/solution.py
@@ -322,12 +322,6 @@
     takes_high = jnp.logical_and(a == N_ANG - 1, g < n_gx - 1)
     takes = jnp.logical_or(takes_low, takes_high)
 
-    def send_answered(which):
-        @pl.when(jnp.logical_and(which, up_right))
-        def _():
-            pl.semaphore_wait(ready_right, 1)
-            edge_copy(True, a, (0, y, g + 1)).start()
-
     part_copy(2, 0).start()
     part_copy(2, 1).start()
 
@@ -359,19 +353,13 @@
         pl.semaphore_wait(ready_left, 1)
         edge_copy(False, a, (N_ANG - 1, y, g - 1)).start()
 
-    send_answered(takes)
-
-    @pl.when(takes)
-    def _():
-        for place in range(N_ANG):
-            edge_copy(True, place, (0, y, g)).wait_recv()
-        at_low = lax.broadcasted_iota(jnp.int32, (16, 8, 128), 2) < 64
-        shown = jnp.logical_xor(at_low, takes_low)
-        field_edge[...] = jnp.where(shown, field_edge[...], 0.0)
-        for half in range(2):
-            extra[:, pl.ds(8 * half, 8), :] = jnp.swapaxes(
-                field_edge[pl.ds(8 * half, 8)], 0, 1
-            )
+    def send_answered(which):
+        @pl.when(which)
+        def _():
+            pl.semaphore_wait(ready_right, 1)
+            edge_copy(True, a, (0, y, g + 1)).start()
+
+    send_answered(g == middle - 1)
 
     for d in range(1, N_ANG):
         strip_copy(d).wait_recv()
@@ -405,22 +393,48 @@
             total = (part_send[0, lines] + part_recv[1, lines]) + (
                 part_recv[3, lines] + part_recv[2, lines]
             )
-            beside = extra[i]
             scaled[HALO + i, :, 0:256] = total * -unit
-            scaled[HALO + i, :, 256:384] = (beside + beside) - unit * turned[lines]
+            scaled[HALO + i, :, 256:384] = turned[lines] * -unit
         if h == 0:
 
-            @pl.when(y > 0)
+            @pl.when(jnp.logical_and(y > 0, jnp.logical_not(takes)))
             def _():
                 below.start()
 
         else:
 
-            @pl.when(y < n_gy - 1)
+            @pl.when(jnp.logical_and(y < n_gy - 1, jnp.logical_not(takes)))
             def _():
                 above.start()
 
-    send_answered(jnp.logical_not(takes))
+    send_answered(g < middle - 1)
+
+    @pl.when(takes)
+    def _():
+        for place in range(N_ANG):
+            edge_copy(True, place, (0, y, g)).wait_recv()
+        at_low = lax.broadcasted_iota(jnp.int32, (16, 8, 128), 2) < 64
+        shown = jnp.logical_xor(at_low, takes_low)
+        field_edge[...] = jnp.where(shown, field_edge[...], 0.0)
+        for half in range(2):
+            extra[:, pl.ds(8 * half, 8), :] = jnp.swapaxes(
+                field_edge[pl.ds(8 * half, 8)], 0, 1
+            )
+
+    @pl.when(takes)
+    def _():
+        for i in range(8):
+            beside = extra[i]
+            own_edge = scaled[HALO + i, :, 256:384]
+            scaled[HALO + i, :, 256:384] = own_edge + (beside + beside)
+
+    @pl.when(jnp.logical_and(y > 0, takes))
+    def _():
+        below.start()
+
+    @pl.when(jnp.logical_and(y < n_gy - 1, takes))
+    def _():
+        above.start()
 
     lane = lax.broadcasted_iota(jnp.int32, (16, 384), 1)
     plane = lax.broadcasted_iota(jnp.int32, (16, 384), 0)

time: 27.2 us -> 24.7 us (0.908)
  the two profiles are of different devices: /device:TPU:360 before, /device:TPU:259 now
where the time goes in v4:
time: 24.7 us; the launch traced here: 24.6 us
  Pallas kernels  23.9 us (97%)
  local copies, waits for them, and re-layouts  0.66 us (3%)
    pallas_call x1, Pallas kernels, per_device(): pl.pallas_call(functools.partial(body, sizes), name='laminography', out_s...  23.9 us
    unnamed x1, local copies, waits for them, and re-layouts  0.66 us

profile of v4, /device:TPU:259, one launch (start us, length us, event | category | flops | bytes accessed | tf_op | source)
XLA Modules:
  0.0 24.6 jit_solution(3335067918892668911)
XLA Ops:
  0.0 23.9 %laminography.1 = f32[4,8,1024]{2,1,0:T(8,128)S(1)} custom-call(bf16[256,512]{1,0:T(8,128)(2,1)} %bitcast.3, s32[1,512]{1,0:T(1,128)} %bitcast.4, s32[1,512]{1,0:T(1,128)} %bitcast.5, f32[4,512]{1,0:T(4,128)} %taps_hbm.1, f32[1500]{0:T(1024)} %weights_hbm.1, f32[4,8,1024]{2,1,0:T(8,128)} %volume_hbm.1, f32[4,8,1024]{2,1,0:T(8,128)} %multiplier_hbm.1, ...), custom_call_target="tpu_custom_call" | custom-call | tf_op jit(solution)/shard_map/laminography/pallas_call | solution.py:601
  23.9 0.7 %copy.11 = f32[4,8,1024]{2,1,0:T(8,128)} copy(f32[4,8,1024]{2,1,0:T(8,128)S(1)} %laminography.1) | data formatting | bytes 262144
